TPU v7x, 512 devices: a whole 4x4x16 slice. The times are simulated.
512 devices in a mesh: par: 64 (over x, z), obs: 8 (over y, core).
Axes of the slice: x: 4, y: 4, z: 16, core: 2. Of those that a mesh axis runs over, the one named last changes fastest.
Arguments:
- unscaled_tile_values: bfloat16 [128, 8, 1024, 1024], P('par', 'obs'), may hold values from -0.046875 to 0.046875
- tile_observe_row: int32 [128, 8], P('par', 'obs'), may hold values from 0 to 1
- tile_param_block: int32 [128, 8], P('par', 'obs'), may hold values from 0 to 1
- tile_scale_exponent: int32 [128, 8], P('par', 'obs'), may hold values from -1 to 2
- tile_count: int32 [64, 8], P('par', 'obs'), may hold values from 0 to 2, as said below
- probes: bfloat16 [131072, 64], P(('par', 'obs')), may hold values from -6 to 6
- noise_weight: float32 [16384], P('obs'), may hold values from 0.25 to 4
Outputs:
- range_basis: float32 [131072, 64], P(('par', 'obs'))
Inputs may be any that keep to these rules, and one draw needn't show every extreme that they name: `tile_count`: some device has all 2 slots live in every draw; many have none.
All inputs are finite; a program needn't handle non-finite values.
Results may differ from a plain program's by a relative error of at most 0.0027.
Values may be sent and summed in bfloat16 or wider, within the bound.
No kernel may reach another device: no remote copies, remote signals or barrier semaphores. Data moves between devices by JAX's collectives and lax.ppermute only.
A program may use at most 64 MiB of HBM per device.

v0:
```python
import jax
import jax.numpy as jnp
from jax import lax
from jax.sharding import PartitionSpec as P


def shards(
    unscaled_tile_values,
    tile_observe_row,
    tile_param_block,
    tile_scale_exponent,
    tile_count,
    probes,
    noise_weight,
):
    slots = unscaled_tile_values.shape[0]
    side = unscaled_tile_values.shape[-1]
    width = probes.shape[1]
    obs_rows = noise_weight.shape[0]
    live_count = tile_count[0, 0]
    panels = lax.all_gather(probes, "obs", axis=0, tiled=True)
    forward = jnp.zeros((obs_rows, width), jnp.float32)
    for kslot in range(slots):
        matrix = unscaled_tile_values[kslot, 0]
        scale = jnp.exp2(tile_scale_exponent[kslot, 0].astype(jnp.float32))
        row_start = tile_observe_row[kslot, 0] * side
        col_start = tile_param_block[kslot, 0] * side
        panel = lax.dynamic_slice_in_dim(panels, col_start, side, 0)

        def live_product(matrix=matrix, panel=panel, scale=scale):
            return jnp.dot(matrix, panel, preferred_element_type=jnp.float32) * scale

        def dead_product():
            return jnp.zeros((side, width), jnp.float32)

        product = lax.cond(kslot < live_count, live_product, dead_product)
        current = lax.dynamic_slice_in_dim(forward, row_start, side, 0)
        forward = lax.dynamic_update_slice_in_dim(forward, current + product, row_start, 0)
    summed = lax.psum(forward, "par")
    weighted = (noise_weight[:, None] * summed).astype(jnp.bfloat16)
    result = jnp.zeros((panels.shape[0], width), jnp.float32)
    for kslot in range(slots):
        matrix = unscaled_tile_values[kslot, 0]
        scale = jnp.exp2(tile_scale_exponent[kslot, 0].astype(jnp.float32))
        row_start = tile_observe_row[kslot, 0] * side
        col_start = tile_param_block[kslot, 0] * side
        rows = lax.dynamic_slice_in_dim(weighted, row_start, side, 0)

        def live_back(matrix=matrix, rows=rows, scale=scale):
            return (
                lax.dot_general(
                    matrix, rows, (((0,), (0,)), ((), ())), preferred_element_type=jnp.float32
                )
                * scale
            )

        def dead_back():
            return jnp.zeros((side, width), jnp.float32)

        product = lax.cond(kslot < live_count, live_back, dead_back)
        current = lax.dynamic_slice_in_dim(result, col_start, side, 0)
        result = lax.dynamic_update_slice_in_dim(result, current + product, col_start, 0)
    return lax.psum_scatter(result, "obs", scatter_dimension=0, tiled=True)


def solution(mesh):
    in_specs = (
        P("par", "obs", None, None),
        P("par", "obs"),
        P("par", "obs"),
        P("par", "obs"),
        P("par", "obs"),
        P(("par", "obs"), None),
        P("obs"),
    )
    out_specs = P(("par", "obs"), None)
    return jax.shard_map(shards, mesh=mesh, in_specs=in_specs, out_specs=out_specs, check_vma=False)
```

profile of v0, /device:TPU:1, one launch (start us, length us, event | category | flops | bytes accessed | tf_op | source)
XLA Modules:
  0.0 350.6 jit_solution(6969131610074075867)
XLA Ops:
  6.5 0.0 all-reduce.2.cloned.1.call-start
  6.5 1.3 fusion.13
  8.4 1.4 fusion.14
  11.7 0.0 copy-start.4
  11.7 0.0 copy-start.2
  11.7 4.0 %slice_bitcast_fusion = (bf16[1024,1024]{1,0:T(8,128)(2,1)S(1)}, bf16[1024,1024]{1,0:T(8,128)(2,1)}) fusion(bf16[2,1,1024,1024]{3,2,1,0:T(8,128)(2,1)} %param.15), kind=kLoop, calls=%fused_computation.16 | loop fusion | bytes 8388608 | tf_op jit(solution)/shard_map/squeeze | solution.py:24
  15.7 0.0 copy-done.4
  15.7 0.7 fusion.12
  17.1 0.0 copy-done.2
  17.1 0.1 copy.8
  17.2 19.8 %all_gather.3 = bf16[2048,64]{1,0:T(8,128)(2,1)S(1)} all-gather(bf16[256,64]{1,0:T(8,128)(2,1)S(1)} %copy.8), channel_id=1, replica_groups=mesh['par'=64,'obs'=8] {'obs'}, dimensions={0}, use_global_device_ids=true | all-gather | bytes 294912 | tf_op jit(solution)/shard_map/all_gather | solution.py:21
  38.6 0.0 copy-start.3
  38.6 0.1 add_dynamic-update-slice_fusion.1
  38.7 0.0 copy-start.1
  38.7 0.8 copy-done.1
  39.5 0.0 all-reduce.2.cloned.1.call-update
  39.5 0.0 reduce-scatter.2.cloned.1.call-start
  39.6 256.6 %all-reduce.2.cloned.1.call-done = f32[2048,64]{0,1:T(8,128)} async-done(((f32[2048,64]{0,1:T(8,128)}), f32[2048,64]{0,1:T(8,128)}) %all-reduce.2.cloned.1.call-update) | async-done | bytes 524304 | tf_op jit(solution)/shard_map/psum | solution.py:39
  296.2 0.0 copy-done.3
  296.2 1.1 multiply_convert_fusion
  297.4 0.7 conditional.7
  297.4 0.7 broadcast.22
  298.1 1.0 add_dynamic-update-slice_fusion
  299.1 0.0 copy-start
  299.1 0.8 copy-done
  299.9 0.0 reduce-scatter.2.cloned.1.call-update
  299.9 43.9 %reduce-scatter.2.cloned.1.call-done = f32[256,64]{0,1:T(8,128)} async-done(((f32[2048,64]{0,1:T(8,128)}), f32[256,64]{0,1:T(8,128)}) %reduce-scatter.2.cloned.1.call-update) | async-done | bytes 65552 | tf_op jit(solution)/shard_map/reduce_scatter | solution.py:63
  (10 shorter events, 0.3 us)
Async XLA Ops:
  6.5 289.6 %all-reduce.2.cloned.1.call-start = ((), (), s32[]{:S(2)}) async-start(), calls=%async_computation.1 | async-start | bytes 1048576 | tf_op jit(solution)/shard_map/psum | solution.py:39
  11.7 4.0 %copy-start.4 = (s32[2,1]{0,1:T(1,128)S(1)}, s32[2,1]{0,1:T(1,128)}, u32[]{:S(2)}) copy-start(s32[2,1]{0,1:T(1,128)} %param.18) | copy-start | bytes 28
  11.7 5.4 %copy-start.2 = (bf16[256,64]{0,1:T(8,128)(2,1)S(1)}, bf16[256,64]{0,1:T(8,128)(2,1)}, u32[]{:S(2)}) copy-start(bf16[256,64]{0,1:T(8,128)(2,1)} %param.20) | copy-start | bytes 98308
  38.6 257.6 %copy-start.3 = (f32[2048]{0:T(1024)S(1)}, f32[2048]{0:T(1024)}, u32[]{:S(2)}) copy-start(f32[2048]{0:T(1024)} %param.21) | copy-start | bytes 24580
  38.7 0.8 copy-start.1
  39.5 304.3 %reduce-scatter.2.cloned.1.call-start = ((), (), s32[]{:S(2)}) async-start(), calls=%async_computation.2 | async-start | bytes 589824 | tf_op jit(solution)/shard_map/reduce_scatter | solution.py:63
  299.1 0.8 copy-start
Sparse Core Ops, SparseCore 0:
  39.6 256.4 all-reduce.1
  300.0 43.7 reduce-scatter.1
where the time goes:
time: 352 us; the launch traced here: 351 us
  waiting for transfers between devices  301 us (86%)
  blocking collectives  19.8 us (6%)
  between operations  18.1 us (5%)
  local copies, waits for them, and re-layouts  9.98 us (3%)
    psum x1, waiting for transfers between devices, shards(): summed = lax.psum(forward, 'par')  257 us
    reduce_scatter x1, waiting for transfers between devices, shards(): return lax.psum_scatter(result, 'obs', scatter_dimension=0, tiled=True)  43.9 us
    all_gather x1, blocking collectives, shards(): panels = lax.all_gather(probes, 'obs', axis=0, tiled=True)  19.8 us
  transfers between devices with their start and end apart: 2, of which 2 were waited for; matrix products, arithmetic and copies ran while one was open for 0% of the time, Pallas kernels for 0%

commit v1 on v0

v1 whole, which is shorter than its diff:
```python
import jax
import jax.numpy as jnp
from jax import lax
from jax.sharding import Mesh, PartitionSpec as P

OBS = ("y", "core")
PAR = ("x", "zh", "zl")
NEAR = ("x", "zl")


def exchange(pieces, axes):
    return lax.all_to_all(pieces, axes, 0, 0, tiled=True)


def shards(
    unscaled_tile_values,
    tile_observe_row,
    tile_param_block,
    tile_scale_exponent,
    tile_count,
    probes,
    noise_weight,
):
    slots = unscaled_tile_values.shape[0]
    side = unscaled_tile_values.shape[-1]
    own, width = probes.shape
    n_obs = lax.axis_size(OBS)
    n_near = lax.axis_size(NEAR)
    obs_rows = noise_weight.shape[0]
    piece = obs_rows // n_near
    live_count = tile_count[0, 0]

    panels = exchange(jnp.broadcast_to(probes.T, (n_obs, width, own)), OBS)
    panels = panels.transpose(1, 0, 2).reshape(width, n_obs * own)

    forward = jnp.zeros((width, obs_rows), jnp.float32)
    for k in range(slots):
        scale = jnp.exp2(tile_scale_exponent[k, 0].astype(jnp.float32))
        row = tile_observe_row[k, 0] * side
        col = tile_param_block[k, 0] * side

        def live_product(k=k, col=col, scale=scale):
            panel = lax.dynamic_slice_in_dim(panels, col, side, 1)
            return scale * lax.dot_general(
                panel,
                unscaled_tile_values[k, 0],
                (((1,), (1,)), ((), ())),
                preferred_element_type=jnp.float32,
            )

        def dead_product():
            return jnp.zeros((width, side), jnp.float32)

        product = lax.cond(k < live_count, live_product, dead_product)
        current = lax.dynamic_slice_in_dim(forward, row, side, 1)
        forward = lax.dynamic_update_slice_in_dim(forward, current + product, row, 1)

    pieces = forward.reshape(width, n_near, piece).transpose(1, 0, 2)
    partial = exchange(pieces, NEAR).sum(0)
    total = lax.all_gather(partial, "zh").sum(0)
    here = lax.axis_index(NEAR)
    noise = lax.dynamic_slice_in_dim(noise_weight, here * piece, piece, 0)
    part = (noise[None, :] * total).astype(jnp.bfloat16)
    weighted = exchange(jnp.broadcast_to(part, (n_near, width, piece)), NEAR)
    weighted = weighted.transpose(1, 0, 2).reshape(width, obs_rows)

    result = jnp.zeros((width, n_obs * own), jnp.float32)
    for k in range(slots):
        scale = jnp.exp2(tile_scale_exponent[k, 0].astype(jnp.float32))
        row = tile_observe_row[k, 0] * side
        col = tile_param_block[k, 0] * side

        def live_back(k=k, row=row, scale=scale):
            rows = lax.dynamic_slice_in_dim(weighted, row, side, 1)
            return scale * jnp.dot(
                rows, unscaled_tile_values[k, 0], preferred_element_type=jnp.float32
            )

        def dead_back():
            return jnp.zeros((width, side), jnp.float32)

        product = lax.cond(k < live_count, live_back, dead_back)
        current = lax.dynamic_slice_in_dim(result, col, side, 1)
        result = lax.dynamic_update_slice_in_dim(result, current + product, col, 1)
    pieces = result.astype(jnp.bfloat16).reshape(width, n_obs, own).transpose(1, 0, 2)
    summed = exchange(pieces, OBS).astype(jnp.float32).sum(0)
    return summed.T


def solution(mesh):
    near = 4
    n_par, n_obs = mesh.devices.shape
    n_x = 4
    devices = mesh.devices.reshape(n_x, n_par // n_x // near, near, n_obs // 2, 2)
    split = Mesh(devices, PAR + OBS)
    in_specs = (
        P(PAR, OBS, None, None),
        P(PAR, OBS),
        P(PAR, OBS),
        P(PAR, OBS),
        P(PAR, OBS),
        P(PAR + OBS, None),
        P(OBS),
    )
    out_specs = P(PAR + OBS, None)
    return jax.shard_map(shards, mesh=split, in_specs=in_specs, out_specs=out_specs, check_vma=False)
```

time: 352 us -> 99.2 us (0.28)
  waiting for transfers between devices: 301 us -> 22.9 us
  starting transfers between devices: 0.04 us -> 21 us
  blocking collectives: 19.8 us -> 39.9 us
  between operations: 18.1 us -> 4.81 us
    psum x1 -> x0, waiting for transfers between devices: 257 us -> none  [shards(): summed = lax.psum(forward, 'par')]
    reduce_scatter x1 -> x0, waiting for transfers between devices: 43.9 us -> none  [shards(): return lax.psum_scatter(result, 'obs', scatter_dimension=0, tiled=True)]
    all_to_all x0 -> x3, waiting for transfers between devices: none -> 22.9 us  [exchange(): return lax.all_to_all(pieces, axes, 0, 0, tiled=True)]
    all_to_all x0 -> x3, starting transfers between devices: none -> 21 us  [exchange(): return lax.all_to_all(pieces, axes, 0, 0, tiled=True)]
    all_to_all x0 -> x1, blocking collectives: none -> 17.4 us  [exchange(): return lax.all_to_all(pieces, axes, 0, 0, tiled=True)]
    squeeze x1 -> x0, local copies, waits for them, and re-layouts: 4.01 us -> none  [shards(): matrix = unscaled_tile_values[kslot, 0]]
  transfers between devices with their start and end apart: 2 -> 3, of which waited for: 2 -> 2; matrix products, arithmetic and copies ran while one was open for 0% -> 5% of each run, Pallas kernels for 0% -> 0%
where the time goes in v1:
time: 99.2 us; the launch traced here: 98 us
  blocking collectives  39.9 us (40%)
  waiting for transfers between devices  22.9 us (23%)
  starting transfers between devices  21 us (21%)
  local copies, waits for them, and re-layouts  8.4 us (8%)
  between operations  4.81 us (5%)
    all_to_all x3, waiting for transfers between devices, exchange(): return lax.all_to_all(pieces, axes, 0, 0, tiled=True)  22.9 us
    all_gather x1, blocking collectives, shards(): total = lax.all_gather(partial, 'zh').sum(0)  22.6 us
    all_to_all x3, starting transfers between devices, exchange(): return lax.all_to_all(pieces, axes, 0, 0, tiled=True)  21 us
    all_to_all x1, blocking collectives, exchange(): return lax.all_to_all(pieces, axes, 0, 0, tiled=True)  17.4 us
  transfers between devices with their start and end apart: 3, of which 2 were waited for; matrix products, arithmetic and copies ran while one was open for 5% of the time, Pallas kernels for 0%

profile of v1, /device:TPU:1, one launch (start us, length us, event | category | flops | bytes accessed | tf_op | source)
XLA Modules:
  0.0 98.0 jit_solution(13972171814485923331)
XLA Ops:
  0.0 1.5 %broadcast_in_dim.7 = bf16[8,64,256]{2,1,0:T(8,128)(2,1)} broadcast(bf16[64,256]{1,0:T(8,128)(2,1)} %bitcast.56), dimensions={1,2} | broadcast | bytes 294912 | tf_op jit(solution)/shard_map/broadcast_in_dim | solution.py:33
  1.5 10.2 %all-to-all-start = ((bf16[8,64,256]{2,1,0:T(8,128)(2,1)}), bf16[8,64,256]{2,1,0:T(8,128)(2,1)S(1)}, u32[]{:S(2)}, u32[]{:S(2)}) async-start(bf16[8,64,256]{2,1,0:T(8,128)(2,1)} %broadcast_in_dim.7), calls=%async_computation | async-start | bytes 524288 | tf_op jit(solution)/shard_map/all_to_all | solution.py:12
  11.7 1.3 %fusion.34 = (s32[1,1]{0,1:T(1,128)}, s32[1,1]{0,1:T(1,128)}) fusion(s32[2,1]{0,1:T(1,128)} %param.16), kind=kLoop, calls=%fused_computation.33 | loop fusion | bytes 16 | tf_op jit(solution)/shard_map/slice | solution.py:39
  14.3 1.3 %fusion.32 = (s32[1,1]{0,1:T(1,128)}, s32[1,1]{0,1:T(1,128)}) fusion(s32[2,1]{0,1:T(1,128)} %param.17), kind=kLoop, calls=%fused_computation.31 | loop fusion | bytes 16 | tf_op jit(solution)/shard_map/slice | solution.py:40
  16.2 1.4 %fusion.33 = (s32[1,1]{0,1:T(1,128)}, s32[1,1]{0,1:T(1,128)}) fusion(s32[2,1]{0,1:T(1,128)} %param.18), kind=kLoop, calls=%fused_computation.32 | loop fusion | bytes 16 | tf_op jit(solution)/shard_map/slice | solution.py:38
  20.3 0.0 all-to-all-done
  20.5 0.1 add_dynamic-update-slice_fusion.1
  20.6 0.1 copy.18
  20.7 1.0 copy.13
  21.6 7.3 %all-to-all-start.1 = ((f32[16,64,128]{2,1,0:T(8,128)}), f32[16,64,128]{2,1,0:T(8,128)S(1)}, u32[]{:S(2)}, u32[]{:S(2)}) async-start(f32[16,64,128]{2,1,0:T(8,128)} %copy.13), calls=%async_computation.1 | async-start | bytes 1048576 | tf_op jit(solution)/shard_map/all_to_all | solution.py:12
  28.9 0.8 dynamic_slice.21
  29.7 14.9 %all-to-all-done.1 = f32[16,64,128]{2,1,0:T(8,128)S(1)} async-done(((f32[16,64,128]{2,1,0:T(8,128)}), f32[16,64,128]{2,1,0:T(8,128)S(1)}, u32[]{:S(2)}, u32[]{:S(2)}) %all-to-all-start.1) | async-done | bytes 524320 | tf_op jit(solution)/shard_map/all_to_all | solution.py:12
  44.7 22.6 %all-gather = f32[256,128]{1,0:T(8,128)S(1)} all-gather(f32[64,128]{1,0:T(8,128)S(1)} %reduce_sum.27), channel_id=2, replica_groups=mesh['x'=4,'zh'=4,'zl'=4,'y'=4,'core'=2] {'zh'}, dimensions={0}, use_global_device_ids=true | all-gather | bytes 163840 | tf_op jit(solution)/shard_map/all_gather | solution.py:60
  67.3 0.7 broadcast_in_dim.8
  68.0 3.5 %all-to-all-start.2 = ((bf16[16,64,128]{2,1,0:T(8,128)(2,1)}), bf16[16,64,128]{2,1,0:T(8,128)(2,1)S(1)}, u32[]{:S(2)}, u32[]{:S(2)}) async-start(bf16[16,64,128]{2,1,0:T(8,128)(2,1)} %broadcast_in_dim.8), calls=%async_computation.2 | async-start | bytes 524288 | tf_op jit(solution)/shard_map/all_to_all | solution.py:12
  71.6 8.0 %all-to-all-done.2 = bf16[16,64,128]{2,1,0:T(8,128)(2,1)S(1)} async-done(((bf16[16,64,128]{2,1,0:T(8,128)(2,1)}), bf16[16,64,128]{2,1,0:T(8,128)(2,1)S(1)}, u32[]{:S(2)}, u32[]{:S(2)}) %all-to-all-start.2) | async-done | bytes 262176 | tf_op jit(solution)/shard_map/all_to_all | solution.py:12
  79.7 0.1 add_dynamic-update-slice_fusion
  79.8 0.1 copy.19
  80.0 17.4 %all_to_all.20 = bf16[8,64,256]{2,1,0:T(8,128)(2,1)S(1)} all-to-all(bf16[8,64,256]{2,1,0:T(8,128)(2,1)S(1)} %copy.15), channel_id=1, replica_groups=mesh['x'=4,'zh'=4,'zl'=4,'y'=4,'core'=2] {'y','core'}, dimensions={0} | all-to-all | bytes 524288 | tf_op jit(solution)/shard_map/all_to_all | solution.py:12
  97.3 0.7 convert_reduce_fusion
  (19 shorter events, 0.5 us)
Async XLA Ops:
  1.5 18.8 %all-to-all-start = ((bf16[8,64,256]{2,1,0:T(8,128)(2,1)}), bf16[8,64,256]{2,1,0:T(8,128)(2,1)S(1)}, u32[]{:S(2)}, u32[]{:S(2)}) async-start(bf16[8,64,256]{2,1,0:T(8,128)(2,1)} %broadcast_in_dim.7), calls=%async_computation | async-start | bytes 524288 | tf_op jit(solution)/shard_map/all_to_all | solution.py:12
  21.6 23.0 %all-to-all-start.1 = ((f32[16,64,128]{2,1,0:T(8,128)}), f32[16,64,128]{2,1,0:T(8,128)S(1)}, u32[]{:S(2)}, u32[]{:S(2)}) async-start(f32[16,64,128]{2,1,0:T(8,128)} %copy.13), calls=%async_computation.1 | async-start | bytes 1048576 | tf_op jit(solution)/shard_map/all_to_all | solution.py:12
  68.0 11.5 %all-to-all-start.2 = ((bf16[16,64,128]{2,1,0:T(8,128)(2,1)}), bf16[16,64,128]{2,1,0:T(8,128)(2,1)S(1)}, u32[]{:S(2)}, u32[]{:S(2)}) async-start(bf16[16,64,128]{2,1,0:T(8,128)(2,1)} %broadcast_in_dim.8), calls=%async_computation.2 | async-start | bytes 524288 | tf_op jit(solution)/shard_map/all_to_all | solution.py:12

commit v2 on v1

v2 whole, which is shorter than its diff:
```python
import jax
import jax.numpy as jnp
from jax import lax
from jax.experimental import pallas as pl
from jax.experimental.pallas import tpu as pltpu
from jax.sharding import Mesh, PartitionSpec as P

OBS = ("y", "core")
PAR = ("x", "zh", "zl")
NEAR = ("x", "zl")
VMEM = pl.BlockSpec(memory_space=pltpu.VMEM)
SMEM = pl.BlockSpec(memory_space=pltpu.SMEM)
HBM = pl.BlockSpec(memory_space=pltpu.HBM)
PARAMS = pltpu.CompilerParams(vmem_limit_bytes=32 * 2**20)
BAND = 256


def exchange(pieces, axes):
    return lax.all_to_all(pieces, axes, 0, 0, tiled=True)


def in_hbm(array):
    return pltpu.with_memory_space_constraint(array, pltpu.HBM)


def call(kernel, out, in_specs, *args, out_specs=VMEM, scratch=()):
    return pl.pallas_call(
        kernel,
        out_shape=out,
        in_specs=in_specs,
        out_specs=out_specs,
        scratch_shapes=list(scratch),
        compiler_params=PARAMS,
    )(*args)


def power(exponent):
    return lax.shift_left(jnp.int32(1), exponent + 1).astype(jnp.float32) * 0.5


def start_kernel(count, row, col, exponent, probes, copies, info, arrived):
    sent = [
        pltpu.make_async_copy(probes, copies.at[i], arrived.at[i]) for i in range(copies.shape[0])
    ]
    for copy in sent:
        copy.start()
    slots = row.shape[1]
    info[0] = count[0, 0]
    for k in range(slots):
        info[1 + k] = row[0, k]
        info[1 + slots + k] = col[0, k]
        info[1 + 2 * slots + k] = exponent[0, k]
    for copy in sent:
        copy.wait()


def slot_info(info, k, slots):
    scale = power(info[1 + 2 * slots + k])
    return k < info[0], info[1 + k], info[1 + slots + k], scale


def load_bands(tiles, held, arrived):
    slots, _, side, _ = tiles.shape
    loads = {}
    for k in range(slots):
        for j in range(side // BAND):
            band = pl.ds(BAND * j, BAND)
            loads[k, j] = pltpu.make_async_copy(
                tiles.at[k, 0, band], held.at[k, band], arrived.at[k, j]
            )
            loads[k, j].start()
    return loads


def forward_kernel(info, panels, tiles, out, held, arrived):
    loads = load_bands(tiles, held, arrived)
    slots, side, _ = held.shape
    own, piece = panels.shape[2], out.shape[2]
    per_col, per_row, per_band = side // own, side // piece, BAND // piece
    out[...] = jnp.zeros_like(out)
    for k in range(slots):
        live, row, col, scale = slot_info(info, k, slots)
        for j in range(side // BAND):
            loads[k, j].wait()

            @pl.when(live)
            def _(j=j, k=k, row=row, col=col, scale=scale):
                panel = jnp.concatenate([panels[col * per_col + i] for i in range(per_col)], axis=1)
                product = scale * lax.dot_general(
                    panel,
                    held[k, pl.ds(BAND * j, BAND), :],
                    (((1,), (1,)), ((), ())),
                    preferred_element_type=jnp.float32,
                )
                for t in range(per_band):
                    where = row * per_row + j * per_band + t
                    out[where] = out[where] + product[:, t * piece : (t + 1) * piece]


def weigh_kernel(sums, noise, out):
    here = lax.axis_index(NEAR)
    total = sums[0]
    for i in range(1, sums.shape[0]):
        total = total + sums[i]
    weighted = (noise[pl.ds(here, 1), :] * total).astype(jnp.bfloat16)
    for i in range(out.shape[0]):
        out[i] = weighted


def back_kernel(info, weighted, tiles, out, total, held, arrived):
    loads = load_bands(tiles, held, arrived)
    slots, side, _ = held.shape
    piece, own = weighted.shape[2], out.shape[2]
    per_col, per_row, per_band = side // own, side // piece, BAND // piece
    total[...] = jnp.zeros_like(total)
    for k in range(slots):
        live, row, col, scale = slot_info(info, k, slots)
        for j in range(side // BAND):
            loads[k, j].wait()

            @pl.when(live)
            def _(j=j, k=k, row=row, col=col, scale=scale):
                first = row * per_row + j * per_band
                rows = jnp.concatenate([weighted[first + i] for i in range(per_band)], axis=1)
                product = scale * jnp.dot(
                    rows,
                    held[k, pl.ds(BAND * j, BAND), :],
                    preferred_element_type=jnp.float32,
                )
                for t in range(per_col):
                    where = col * per_col + t
                    total[where] = total[where] + product[:, t * own : (t + 1) * own]

    out[...] = total[...].astype(jnp.bfloat16)


def shards(
    unscaled_tile_values,
    tile_observe_row,
    tile_param_block,
    tile_scale_exponent,
    tile_count,
    probes,
    noise_weight,
):
    own, width = probes.shape
    n_obs = lax.axis_size(OBS)
    n_near = lax.axis_size(NEAR)
    piece = noise_weight.shape[0] // n_near
    slots, _, side, _ = unscaled_tile_values.shape
    bf16, f32 = jnp.bfloat16, jnp.float32

    copies, info = call(
        start_kernel,
        (pltpu.VMEM((n_obs, width, own), bf16), pltpu.SMEM((1 + 3 * slots,), jnp.int32)),
        [SMEM] * 4 + [HBM],
        tile_count,
        in_hbm(tile_observe_row.T),
        in_hbm(tile_param_block.T),
        in_hbm(tile_scale_exponent.T),
        in_hbm(probes.T),
        out_specs=(VMEM, SMEM),
        scratch=[pltpu.SemaphoreType.DMA((n_obs,))],
    )
    panels = exchange(copies, OBS)
    bands = [
        pltpu.VMEM((slots, side, side), bf16),
        pltpu.SemaphoreType.DMA((slots, side // BAND)),
    ]
    pieces = call(
        forward_kernel,
        pltpu.VMEM((n_near, width, piece), f32),
        [SMEM, VMEM, HBM],
        info,
        panels,
        in_hbm(unscaled_tile_values),
        scratch=bands,
    )
    partial = exchange(pieces, NEAR).sum(0)
    sums = lax.all_gather(partial, "zh")
    weighted = call(
        weigh_kernel,
        pltpu.VMEM((n_near, width, piece), bf16),
        [VMEM] * 2,
        sums,
        noise_weight.reshape(n_near, piece),
    )
    weighted = exchange(weighted, NEAR)
    pieces = call(
        back_kernel,
        pltpu.VMEM((n_obs, width, own), bf16),
        [SMEM, VMEM, HBM],
        info,
        weighted,
        in_hbm(unscaled_tile_values),
        scratch=[pltpu.VMEM((n_obs, width, own), f32)] + bands,
    )
    summed = exchange(pieces, OBS).astype(f32).sum(0)
    return summed.T


def solution(mesh):
    n_par, n_obs = mesh.devices.shape
    devices = mesh.devices.reshape(4, n_par // 16, 4, n_obs // 2, 2)
    split = Mesh(devices, PAR + OBS)
    in_specs = (
        P(PAR, OBS, None, None),
        P(PAR, OBS),
        P(PAR, OBS),
        P(PAR, OBS),
        P(PAR, OBS),
        P(PAR + OBS, None),
        P(OBS),
    )
    out_specs = P(PAR + OBS, None)
    return jax.shard_map(shards, mesh=split, in_specs=in_specs, out_specs=out_specs, check_vma=False)
```

time: 99.2 us -> 90.9 us (0.916)
  blocking collectives: 39.9 us -> 81 us
  waiting for transfers between devices: 22.9 us -> 0 us
  starting transfers between devices: 21 us -> 0 us
  local copies, waits for them, and re-layouts: 8.4 us -> 0.01 us
  Pallas kernels: 0 us -> 8.07 us
  between operations: 4.81 us -> 0.7 us
    all_to_all x1 -> x4, blocking collectives: 17.4 us -> 61 us  [exchange(): return lax.all_to_all(pieces, axes, 0, 0, tiled=True)]
    all_to_all x3 -> x0, waiting for transfers between devices: 22.9 us -> none  [exchange(): return lax.all_to_all(pieces, axes, 0, 0, tiled=True)]
    all_to_all x3 -> x0, starting transfers between devices: 21 us -> none  [exchange(): return lax.all_to_all(pieces, axes, 0, 0, tiled=True)]
    pallas_call x0 -> x4, Pallas kernels: none -> 8.07 us  [call(): pl.pallas_call(kernel, out_shape=out, in_specs=in_specs, out_specs=out_sp...]
    slice x3 -> x0, local copies, waits for them, and re-layouts: 4.01 us -> none  [the longest x1 1.38 us: shards(): scale = jnp.exp2(tile_scale_exponent[k, 0].astype(jnp.float32))]
    all_gather x1, blocking collectives: 22.6 us -> 20 us  [shards(): sums = lax.all_gather(partial, 'zh')]
    broadcast_in_dim x2 -> x0, local copies, waits for them, and re-layouts: 2.21 us -> none  [the longest x1 1.47 us: shards(): panels = exchange(jnp.broadcast_to(probes.T, (n_obs, width, own)), OBS)]
    transpose x2 -> x0, local copies, waits for them, and re-layouts: 1.01 us -> none  [the longest x1 0.97 us: shards(): pieces = forward.reshape(width, n_near, piece).transpose(1, 0, 2)]
  transfers between devices with their start and end apart: 3 -> 0, of which waited for: 2 -> 0; matrix products, arithmetic and copies ran while one was open for 5% -> 0% of each run, Pallas kernels for 0% -> 0%
where the time goes in v2:
time: 90.9 us; the launch traced here: 90.5 us
  blocking collectives  81 us (89%)
  Pallas kernels  8.07 us (9%)
    all_to_all x4, blocking collectives, exchange(): return lax.all_to_all(pieces, axes, 0, 0, tiled=True)  61 us
    all_gather x1, blocking collectives, shards(): sums = lax.all_gather(partial, 'zh')  20 us
    pallas_call x4, Pallas kernels, call(): pl.pallas_call(kernel, out_shape=out, in_specs=in_specs, out_specs=out_sp...  8.07 us

profile of v2, /device:TPU:1, one launch (start us, length us, event | category | flops | bytes accessed | tf_op | source)
XLA Modules:
  0.0 90.5 jit_solution(9173545577433117680)
XLA Ops:
  0.0 0.0 copy-start
  0.7 1.8 %shard_map.73 = (bf16[8,64,256]{2,1,0:T(8,128)(2,1)S(1)}, s32[7]{0:T(128)S(4)}) custom-call(s32[1,1]{1,0:T(1,128)S(6)} %copy.8.count, s32[1,2]{1,0:T(1,128)} %bitcast.10, s32[1,2]{1,0:T(1,128)} %bitcast.11, s32[1,2]{1,0:T(1,128)} %bitcast.12, bf16[64,256]{1,0:T(8,128)(2,1)} %bitcast.9), custom_call_target="tpu_custom_call" | custom-call | tf_op jit(solution)/shard_map/pallas_call | solution.py:27
  2.5 15.8 %all_to_all.20.panels = bf16[8,64,256]{2,1,0:T(8,128)(2,1)S(1)} all-to-all(bf16[8,64,256]{2,1,0:T(8,128)(2,1)S(1)} %get-tuple-element.8), channel_id=1, replica_groups=mesh['x'=4,'zh'=4,'zl'=4,'y'=4,'core'=2] {'y','core'}, dimensions={0} | all-to-all | bytes 524288 | tf_op jit(solution)/shard_map/all_to_all | solution.py:19
  18.3 3.4 %shard_map.74 = f32[16,64,128]{2,1,0:T(8,128)S(1)} custom-call(s32[7]{0:T(128)S(4)} %get-tuple-element.7.info, bf16[8,64,256]{2,1,0:T(8,128)(2,1)S(1)} %all_to_all.20.panels, bf16[2,1,1024,1024]{3,2,1,0:T(8,128)(2,1)} %tiles.3), custom_call_target="tpu_custom_call" | custom-call | tf_op jit(solution)/shard_map/pallas_call | solution.py:27
  21.7 19.9 %all_to_all.21 = f32[16,64,128]{2,1,0:T(8,128)S(1)} all-to-all(f32[16,64,128]{2,1,0:T(8,128)S(1)} %shard_map.74), channel_id=1, replica_groups=mesh['x'=4,'zh'=4,'zl'=4,'y'=4,'core'=2] {'x','zl'}, dimensions={0} | all-to-all | bytes 1048576 | tf_op jit(solution)/shard_map/all_to_all | solution.py:19
  41.6 20.0 %all-gather = f32[256,128]{1,0:T(8,128)S(1)} all-gather(f32[64,128]{1,0:T(8,128)S(1)} %reduce_sum.18), channel_id=2, replica_groups=mesh['x'=4,'zh'=4,'zl'=4,'y'=4,'core'=2] {'zh'}, dimensions={0}, use_global_device_ids=true | all-gather | bytes 163840 | tf_op jit(solution)/shard_map/all_gather | solution.py:180
  61.7 0.0 copy-done
  61.7 11.4 %all_to_all.22.weighted = bf16[16,64,128]{2,1,0:T(8,128)(2,1)S(1)} all-to-all(bf16[16,64,128]{2,1,0:T(8,128)(2,1)S(1)} %shard_map.75), channel_id=1, replica_groups=mesh['x'=4,'zh'=4,'zl'=4,'y'=4,'core'=2] {'x','zl'}, dimensions={0} | all-to-all | bytes 524288 | tf_op jit(solution)/shard_map/all_to_all | solution.py:19
  73.1 2.8 %shard_map.76 = bf16[8,64,256]{2,1,0:T(8,128)(2,1)S(1)} custom-call(s32[7]{0:T(128)S(4)} %get-tuple-element.7.info, bf16[16,64,128]{2,1,0:T(8,128)(2,1)S(1)} %all_to_all.22.weighted, bf16[2,1,1024,1024]{3,2,1,0:T(8,128)(2,1)} %tiles.3), custom_call_target="tpu_custom_call" | custom-call | tf_op jit(solution)/shard_map/pallas_call | solution.py:27
  75.9 13.9 %all_to_all.23 = bf16[8,64,256]{2,1,0:T(8,128)(2,1)S(1)} all-to-all(bf16[8,64,256]{2,1,0:T(8,128)(2,1)S(1)} %shard_map.76), channel_id=1, replica_groups=mesh['x'=4,'zh'=4,'zl'=4,'y'=4,'core'=2] {'y','core'}, dimensions={0} | all-to-all | bytes 524288 | tf_op jit(solution)/shard_map/all_to_all | solution.py:19
  89.8 0.7 convert_reduce_fusion
  (2 shorter events, 0.1 us)
Async XLA Ops:
  0.0 61.7 %copy-start = (f32[2048]{0:T(1024)S(1)}, f32[2048]{0:T(1024)}, u32[]{:S(2)}) copy-start(f32[2048]{0:T(1024)} %param.13) | copy-start | bytes 24580

commit v3 on v2

--- a/solution.py
+++ b/solution.py
@@ -13,6 +13,8 @@
 HBM = pl.BlockSpec(memory_space=pltpu.HBM)
 PARAMS = pltpu.CompilerParams(vmem_limit_bytes=32 * 2**20)
 BAND = 256
+CODE = jnp.int16
+SCALE_ROWS = 16
 
 
 def exchange(pieces, axes):
@@ -38,20 +40,44 @@
     return lax.shift_left(jnp.int32(1), exponent + 1).astype(jnp.float32) * 0.5
 
 
-def start_kernel(count, row, col, exponent, probes, copies, info, arrived):
+def start_kernel(count, row, col, exponent, probes, copies, info, held, arrived, read):
     sent = [
         pltpu.make_async_copy(probes, copies.at[i], arrived.at[i]) for i in range(copies.shape[0])
     ]
+    sent += [
+        pltpu.make_async_copy(source, held.at[i], read.at[i])
+        for i, source in enumerate((row, col, exponent))
+    ]
     for copy in sent:
         copy.start()
+    for copy in sent:
+        copy.wait()
     slots = row.shape[1]
     info[0] = count[0, 0]
-    for k in range(slots):
-        info[1 + k] = row[0, k]
-        info[1 + slots + k] = col[0, k]
-        info[1 + 2 * slots + k] = exponent[0, k]
-    for copy in sent:
-        copy.wait()
+    for i in range(3):
+        for k in range(slots):
+            info[1 + i * slots + k] = held[i, 0, k]
+
+
+def encode(values, out, at):
+    rows = values.shape[0]
+    largest = jnp.max(jnp.abs(values), axis=0, keepdims=True)
+    exponent = jnp.floor(jnp.log2(jnp.maximum(largest, 2.0**-110))) + 1.0
+    codes = jnp.round(values * jnp.exp2(14.0 - exponent))
+    out[(*at, pl.ds(0, rows))] = codes.astype(jnp.int32).astype(CODE)
+    exponent = jnp.broadcast_to(exponent, (SCALE_ROWS, values.shape[1]))
+    out[(*at, pl.ds(rows, SCALE_ROWS))] = exponent.astype(jnp.int32).astype(CODE)
+
+
+def decode(coded):
+    pieces, rows, _ = coded.shape
+    rows -= SCALE_ROWS
+    total = None
+    for i in range(pieces):
+        exponent = coded[i, pl.ds(rows, SCALE_ROWS)].astype(jnp.float32)[:1]
+        part = coded[i, pl.ds(0, rows)].astype(jnp.float32) * jnp.exp2(exponent - 14.0)
+        total = part if total is None else total + part
+    return total
 
 
 def slot_info(info, k, slots):
@@ -72,12 +98,12 @@
     return loads
 
 
-def forward_kernel(info, panels, tiles, out, held, arrived):
+def forward_kernel(info, panels, tiles, out, total, held, arrived):
     loads = load_bands(tiles, held, arrived)
     slots, side, _ = held.shape
     own, piece = panels.shape[2], out.shape[2]
     per_col, per_row, per_band = side // own, side // piece, BAND // piece
-    out[...] = jnp.zeros_like(out)
+    total[...] = jnp.zeros_like(total)
     for k in range(slots):
         live, row, col, scale = slot_info(info, k, slots)
         for j in range(side // BAND):
@@ -94,15 +120,19 @@
                 )
                 for t in range(per_band):
                     where = row * per_row + j * per_band + t
-                    out[where] = out[where] + product[:, t * piece : (t + 1) * piece]
-
-
-def weigh_kernel(sums, noise, out):
+                    total[where] = total[where] + product[:, t * piece : (t + 1) * piece]
+
+    for c in range(out.shape[0]):
+        encode(total[c], out, (c,))
+
+
+def partial_kernel(coded, out):
+    encode(decode(coded), out, ())
+
+
+def weigh_kernel(coded, noise, out):
     here = lax.axis_index(NEAR)
-    total = sums[0]
-    for i in range(1, sums.shape[0]):
-        total = total + sums[i]
-    weighted = (noise[pl.ds(here, 1), :] * total).astype(jnp.bfloat16)
+    weighted = (noise[pl.ds(here, 1), :] * decode(coded)).astype(jnp.bfloat16)
     for i in range(out.shape[0]):
         out[i] = weighted
 
@@ -153,36 +183,42 @@
     copies, info = call(
         start_kernel,
         (pltpu.VMEM((n_obs, width, own), bf16), pltpu.SMEM((1 + 3 * slots,), jnp.int32)),
-        [SMEM] * 4 + [HBM],
+        [SMEM] + [HBM] * 4,
         tile_count,
         in_hbm(tile_observe_row.T),
         in_hbm(tile_param_block.T),
         in_hbm(tile_scale_exponent.T),
         in_hbm(probes.T),
         out_specs=(VMEM, SMEM),
-        scratch=[pltpu.SemaphoreType.DMA((n_obs,))],
+        scratch=[
+            pltpu.SMEM((3, 1, slots), jnp.int32),
+            pltpu.SemaphoreType.DMA((n_obs,)),
+            pltpu.SemaphoreType.DMA((3,)),
+        ],
     )
     panels = exchange(copies, OBS)
     bands = [
         pltpu.VMEM((slots, side, side), bf16),
         pltpu.SemaphoreType.DMA((slots, side // BAND)),
     ]
+    coded = width + SCALE_ROWS
     pieces = call(
         forward_kernel,
-        pltpu.VMEM((n_near, width, piece), f32),
+        pltpu.VMEM((n_near, coded, piece), CODE),
         [SMEM, VMEM, HBM],
         info,
         panels,
         in_hbm(unscaled_tile_values),
-        scratch=bands,
-    )
-    partial = exchange(pieces, NEAR).sum(0)
-    sums = lax.all_gather(partial, "zh")
+        scratch=[pltpu.VMEM((n_near, width, piece), f32)] + bands,
+    )
+    partial = call(
+        partial_kernel, pltpu.VMEM((coded, piece), CODE), [VMEM], exchange(pieces, NEAR)
+    )
     weighted = call(
         weigh_kernel,
         pltpu.VMEM((n_near, width, piece), bf16),
         [VMEM] * 2,
-        sums,
+        lax.all_gather(partial, "zh"),
         noise_weight.reshape(n_near, piece),
     )
     weighted = exchange(weighted, NEAR)

time: 90.9 us -> 86.3 us (0.949)
  blocking collectives: 81 us -> 76.9 us
    all_to_all x4, blocking collectives: 61 us -> 56.6 us  [exchange(): return lax.all_to_all(pieces, axes, 0, 0, tiled=True)]
    pallas_call x4 -> x5, Pallas kernels: 8.07 us -> 7.68 us  [call(): pl.pallas_call(kernel, out_shape=out, in_specs=in_specs, out_specs=out_sp...]
where the time goes in v3:
time: 86.3 us; the launch traced here: 85.9 us
  blocking collectives  76.9 us (89%)
  Pallas kernels  7.68 us (9%)
    all_to_all x4, blocking collectives, exchange(): return lax.all_to_all(pieces, axes, 0, 0, tiled=True)  56.6 us
    all_gather x1, blocking collectives, shards(): lax.all_gather(partial, 'zh')  20.3 us
    pallas_call x5, Pallas kernels, call(): pl.pallas_call(kernel, out_shape=out, in_specs=in_specs, out_specs=out_sp...  7.68 us

profile of v3, /device:TPU:1, one launch (start us, length us, event | category | flops | bytes accessed | tf_op | source)
XLA Modules:
  0.0 85.9 jit_solution(10261451755351834350)
XLA Ops:
  0.0 0.0 copy-start
  0.7 1.2 %shard_map.73 = (bf16[8,64,256]{2,1,0:T(8,128)(2,1)S(1)}, s32[7]{0:T(128)S(4)}) custom-call(s32[1,1]{1,0:T(1,128)S(6)} %copy.8.count, s32[1,2]{1,0:T(1,128)} %bitcast.10, s32[1,2]{1,0:T(1,128)} %bitcast.11, s32[1,2]{1,0:T(1,128)} %bitcast.12, bf16[64,256]{1,0:T(8,128)(2,1)} %bitcast.9), custom_call_target="tpu_custom_call" | custom-call | tf_op jit(solution)/shard_map/pallas_call | solution.py:29
  1.9 15.8 %all_to_all.20.panels = bf16[8,64,256]{2,1,0:T(8,128)(2,1)S(1)} all-to-all(bf16[8,64,256]{2,1,0:T(8,128)(2,1)S(1)} %get-tuple-element.8), channel_id=1, replica_groups=mesh['x'=4,'zh'=4,'zl'=4,'y'=4,'core'=2] {'y','core'}, dimensions={0} | all-to-all | bytes 524288 | tf_op jit(solution)/shard_map/all_to_all | solution.py:21
  17.6 3.5 %shard_map.74 = s16[16,80,128]{2,1,0:T(8,128)(2,1)S(1)} custom-call(s32[7]{0:T(128)S(4)} %get-tuple-element.7.info, bf16[8,64,256]{2,1,0:T(8,128)(2,1)S(1)} %all_to_all.20.panels, bf16[2,1,1024,1024]{3,2,1,0:T(8,128)(2,1)} %tiles.3), custom_call_target="tpu_custom_call" | custom-call | tf_op jit(solution)/shard_map/pallas_call | solution.py:29
  21.2 14.6 %all_to_all.21.coded = s16[16,80,128]{2,1,0:T(8,128)(2,1)S(1)} all-to-all(s16[16,80,128]{2,1,0:T(8,128)(2,1)S(1)} %shard_map.74), channel_id=1, replica_groups=mesh['x'=4,'zh'=4,'zl'=4,'y'=4,'core'=2] {'x','zl'}, dimensions={0} | all-to-all | bytes 655360 | tf_op jit(solution)/shard_map/all_to_all | solution.py:21
  35.7 0.1 shard_map.75
  35.8 20.3 %all-gather = s16[320,128]{1,0:T(8,128)(2,1)S(1)} all-gather(s16[80,128]{1,0:T(8,128)(2,1)S(1)} %shard_map.75), channel_id=2, replica_groups=mesh['x'=4,'zh'=4,'zl'=4,'y'=4,'core'=2] {'zh'}, dimensions={0}, use_global_device_ids=true | all-gather | bytes 102400 | tf_op jit(solution)/shard_map/all_gather | solution.py:221
  56.1 0.0 copy-done
  56.2 11.3 %all_to_all.22.weighted = bf16[16,64,128]{2,1,0:T(8,128)(2,1)S(1)} all-to-all(bf16[16,64,128]{2,1,0:T(8,128)(2,1)S(1)} %shard_map.76), channel_id=1, replica_groups=mesh['x'=4,'zh'=4,'zl'=4,'y'=4,'core'=2] {'x','zl'}, dimensions={0} | all-to-all | bytes 524288 | tf_op jit(solution)/shard_map/all_to_all | solution.py:21
  67.5 2.8 %shard_map.77 = bf16[8,64,256]{2,1,0:T(8,128)(2,1)S(1)} custom-call(s32[7]{0:T(128)S(4)} %get-tuple-element.7.info, bf16[16,64,128]{2,1,0:T(8,128)(2,1)S(1)} %all_to_all.22.weighted, bf16[2,1,1024,1024]{3,2,1,0:T(8,128)(2,1)} %tiles.3), custom_call_target="tpu_custom_call" | custom-call | tf_op jit(solution)/shard_map/pallas_call | solution.py:29
  70.4 14.9 %all_to_all.23 = bf16[8,64,256]{2,1,0:T(8,128)(2,1)S(1)} all-to-all(bf16[8,64,256]{2,1,0:T(8,128)(2,1)S(1)} %shard_map.77), channel_id=1, replica_groups=mesh['x'=4,'zh'=4,'zl'=4,'y'=4,'core'=2] {'y','core'}, dimensions={0} | all-to-all | bytes 524288 | tf_op jit(solution)/shard_map/all_to_all | solution.py:21
  85.3 0.7 convert_reduce_fusion
  (1 shorter events, 0.0 us)
Async XLA Ops:
  0.0 56.1 %copy-start = (f32[2048]{0:T(1024)S(1)}, f32[2048]{0:T(1024)}, u32[]{:S(2)}) copy-start(f32[2048]{0:T(1024)} %param.13) | copy-start | bytes 24580

commit v4 on v3

--- a/solution.py
+++ b/solution.py
@@ -11,7 +11,7 @@
 VMEM = pl.BlockSpec(memory_space=pltpu.VMEM)
 SMEM = pl.BlockSpec(memory_space=pltpu.SMEM)
 HBM = pl.BlockSpec(memory_space=pltpu.HBM)
-PARAMS = pltpu.CompilerParams(vmem_limit_bytes=32 * 2**20)
+PARAMS = pltpu.CompilerParams(vmem_limit_bytes=16 * 2**20)
 BAND = 256
 CODE = jnp.int16
 SCALE_ROWS = 16
@@ -98,7 +98,7 @@
     return loads
 
 
-def forward_kernel(info, panels, tiles, out, total, held, arrived):
+def forward_kernel(info, panels, tiles, out, held, total, arrived):
     loads = load_bands(tiles, held, arrived)
     slots, side, _ = held.shape
     own, piece = panels.shape[2], out.shape[2]
@@ -127,7 +127,9 @@
 
 
 def partial_kernel(coded, out):
-    encode(decode(coded), out, ())
+    encode(decode(coded), out, (0,))
+    for i in range(1, out.shape[0]):
+        out[i] = out[0]
 
 
 def weigh_kernel(coded, noise, out):
@@ -137,29 +139,23 @@
         out[i] = weighted
 
 
-def back_kernel(info, weighted, tiles, out, total, held, arrived):
-    loads = load_bands(tiles, held, arrived)
+def back_kernel(info, weighted, held, out, total):
     slots, side, _ = held.shape
     piece, own = weighted.shape[2], out.shape[2]
-    per_col, per_row, per_band = side // own, side // piece, BAND // piece
+    per_col, per_row = side // own, side // piece
     total[...] = jnp.zeros_like(total)
     for k in range(slots):
         live, row, col, scale = slot_info(info, k, slots)
-        for j in range(side // BAND):
-            loads[k, j].wait()
-
-            @pl.when(live)
-            def _(j=j, k=k, row=row, col=col, scale=scale):
-                first = row * per_row + j * per_band
-                rows = jnp.concatenate([weighted[first + i] for i in range(per_band)], axis=1)
+
+        @pl.when(live)
+        def _(k=k, row=row, col=col, scale=scale):
+            rows = jnp.concatenate([weighted[row * per_row + i] for i in range(per_row)], axis=1)
+            for t in range(per_col):
                 product = scale * jnp.dot(
-                    rows,
-                    held[k, pl.ds(BAND * j, BAND), :],
-                    preferred_element_type=jnp.float32,
+                    rows, held[k, :, pl.ds(own * t, own)], preferred_element_type=jnp.float32
                 )
-                for t in range(per_col):
-                    where = col * per_col + t
-                    total[where] = total[where] + product[:, t * own : (t + 1) * own]
+                where = col * per_col + t
+                total[where] = total[where] + product
 
     out[...] = total[...].astype(jnp.bfloat16)
 
@@ -197,39 +193,42 @@
         ],
     )
     panels = exchange(copies, OBS)
-    bands = [
-        pltpu.VMEM((slots, side, side), bf16),
-        pltpu.SemaphoreType.DMA((slots, side // BAND)),
-    ]
     coded = width + SCALE_ROWS
-    pieces = call(
+    pieces, held = call(
         forward_kernel,
-        pltpu.VMEM((n_near, coded, piece), CODE),
+        (pltpu.VMEM((n_near, coded, piece), CODE), pltpu.VMEM((slots, side, side), bf16)),
         [SMEM, VMEM, HBM],
         info,
         panels,
         in_hbm(unscaled_tile_values),
-        scratch=[pltpu.VMEM((n_near, width, piece), f32)] + bands,
+        out_specs=(VMEM, VMEM),
+        scratch=[
+            pltpu.VMEM((n_near, width, piece), f32),
+            pltpu.SemaphoreType.DMA((slots, side // BAND)),
+        ],
     )
     partial = call(
-        partial_kernel, pltpu.VMEM((coded, piece), CODE), [VMEM], exchange(pieces, NEAR)
+        partial_kernel,
+        pltpu.VMEM((lax.axis_size("zh"), coded, piece), CODE),
+        [VMEM],
+        exchange(pieces, NEAR),
     )
     weighted = call(
         weigh_kernel,
         pltpu.VMEM((n_near, width, piece), bf16),
         [VMEM] * 2,
-        lax.all_gather(partial, "zh"),
+        exchange(partial, "zh"),
         noise_weight.reshape(n_near, piece),
     )
     weighted = exchange(weighted, NEAR)
     pieces = call(
         back_kernel,
         pltpu.VMEM((n_obs, width, own), bf16),
-        [SMEM, VMEM, HBM],
+        [SMEM, VMEM, VMEM],
         info,
         weighted,
-        in_hbm(unscaled_tile_values),
-        scratch=[pltpu.VMEM((n_obs, width, own), f32)] + bands,
+        held,
+        scratch=[pltpu.VMEM((n_obs, width, own), f32)],
     )
     summed = exchange(pieces, OBS).astype(f32).sum(0)
     return summed.T

time: 86.3 us -> 86.8 us (level)
  blocking collectives: 76.9 us -> 79.3 us
  Pallas kernels: 7.68 us -> 5.79 us
    all_to_all x4 -> x5, blocking collectives: 56.6 us -> 79.3 us  [exchange(): return lax.all_to_all(pieces, axes, 0, 0, tiled=True)]
    all_gather x1 -> x0, blocking collectives: 20.3 us -> none  [shards(): lax.all_gather(partial, 'zh')]
    pallas_call x5, Pallas kernels: 7.68 us -> 5.79 us  [call(): pl.pallas_call(kernel, out_shape=out, in_specs=in_specs, out_specs=out_sp...]
where the time goes in v4:
time: 86.8 us; the launch traced here: 86.4 us
  blocking collectives  79.3 us (91%)
  Pallas kernels  5.79 us (7%)
    all_to_all x5, blocking collectives, exchange(): return lax.all_to_all(pieces, axes, 0, 0, tiled=True)  79.3 us
    pallas_call x5, Pallas kernels, call(): pl.pallas_call(kernel, out_shape=out, in_specs=in_specs, out_specs=out_sp...  5.79 us

profile of v4, /device:TPU:1, one launch (start us, length us, event | category | flops | bytes accessed | tf_op | source)
XLA Modules:
  0.0 86.4 jit_solution(8748837544291675000)
XLA Ops:
  0.0 0.0 copy-start
  0.7 1.2 %shard_map.73 = (bf16[8,64,256]{2,1,0:T(8,128)(2,1)S(1)}, s32[7]{0:T(128)S(4)}) custom-call(s32[1,1]{1,0:T(1,128)S(6)} %copy.8.count, s32[1,2]{1,0:T(1,128)} %bitcast.8, s32[1,2]{1,0:T(1,128)} %bitcast.9, s32[1,2]{1,0:T(1,128)} %bitcast.10, bf16[64,256]{1,0:T(8,128)(2,1)} %bitcast.7), custom_call_target="tpu_custom_call" | custom-call | tf_op jit(solution)/shard_map/pallas_call | solution.py:29
  1.9 15.8 %all_to_all.25.panels = bf16[8,64,256]{2,1,0:T(8,128)(2,1)S(1)} all-to-all(bf16[8,64,256]{2,1,0:T(8,128)(2,1)S(1)} %get-tuple-element.10), channel_id=1, replica_groups=mesh['x'=4,'zh'=4,'zl'=4,'y'=4,'core'=2] {'y','core'}, dimensions={0} | all-to-all | bytes 524288 | tf_op jit(solution)/shard_map/all_to_all | solution.py:21
  17.6 3.5 %shard_map.74 = (s16[16,80,128]{2,1,0:T(8,128)(2,1)S(1)}, bf16[2,1024,1024]{2,1,0:T(8,128)(2,1)S(1)}) custom-call(s32[7]{0:T(128)S(4)} %get-tuple-element.9.info, bf16[8,64,256]{2,1,0:T(8,128)(2,1)S(1)} %all_to_all.25.panels, bf16[2,1,1024,1024]{3,2,1,0:T(8,128)(2,1)} %tiles.1), custom_call_target="tpu_custom_call" | custom-call | tf_op jit(solution)/shard_map/pallas_call | solution.py:29
  21.2 14.6 %all_to_all.26.coded = s16[16,80,128]{2,1,0:T(8,128)(2,1)S(1)} all-to-all(s16[16,80,128]{2,1,0:T(8,128)(2,1)S(1)} %get-tuple-element.11), channel_id=1, replica_groups=mesh['x'=4,'zh'=4,'zl'=4,'y'=4,'core'=2] {'x','zl'}, dimensions={0} | all-to-all | bytes 655360 | tf_op jit(solution)/shard_map/all_to_all | solution.py:21
  35.7 0.1 shard_map.75
  35.8 24.2 %all_to_all.27.coded = s16[4,80,128]{2,1,0:T(8,128)(2,1)S(1)} all-to-all(s16[4,80,128]{2,1,0:T(8,128)(2,1)S(1)} %shard_map.75), channel_id=1, replica_groups=mesh['x'=4,'zh'=4,'zl'=4,'y'=4,'core'=2] {'zh'}, dimensions={0} | all-to-all | bytes 163840 | tf_op jit(solution)/shard_map/all_to_all | solution.py:21
  60.0 0.0 copy-done
  60.1 11.4 %all_to_all.28.weighted = bf16[16,64,128]{2,1,0:T(8,128)(2,1)S(1)} all-to-all(bf16[16,64,128]{2,1,0:T(8,128)(2,1)S(1)} %shard_map.76), channel_id=1, replica_groups=mesh['x'=4,'zh'=4,'zl'=4,'y'=4,'core'=2] {'x','zl'}, dimensions={0} | all-to-all | bytes 524288 | tf_op jit(solution)/shard_map/all_to_all | solution.py:21
  71.5 0.9 %shard_map.77 = bf16[8,64,256]{2,1,0:T(8,128)(2,1)S(1)} custom-call(s32[7]{0:T(128)S(4)} %get-tuple-element.9.info, bf16[16,64,128]{2,1,0:T(8,128)(2,1)S(1)} %all_to_all.28.weighted, bf16[2,1024,1024]{2,1,0:T(8,128)(2,1)S(1)} %get-tuple-element.12.held), custom_call_target="tpu_custom_call" | custom-call | tf_op jit(solution)/shard_map/pallas_call | solution.py:29
  72.5 13.3 %all_to_all.29 = bf16[8,64,256]{2,1,0:T(8,128)(2,1)S(1)} all-to-all(bf16[8,64,256]{2,1,0:T(8,128)(2,1)S(1)} %shard_map.77), channel_id=1, replica_groups=mesh['x'=4,'zh'=4,'zl'=4,'y'=4,'core'=2] {'y','core'}, dimensions={0} | all-to-all | bytes 524288 | tf_op jit(solution)/shard_map/all_to_all | solution.py:21
  85.8 0.7 convert_reduce_fusion
  (1 shorter events, 0.0 us)
Async XLA Ops:
  0.0 60.0 %copy-start = (f32[2048]{0:T(1024)S(1)}, f32[2048]{0:T(1024)}, u32[]{:S(2)}) copy-start(f32[2048]{0:T(1024)} %param.13) | copy-start | bytes 24580

commit v5 on v4

--- a/solution.py
+++ b/solution.py
@@ -13,12 +13,14 @@
 HBM = pl.BlockSpec(memory_space=pltpu.HBM)
 PARAMS = pltpu.CompilerParams(vmem_limit_bytes=16 * 2**20)
 BAND = 256
+FIRST_PANELS, FIRST_NEAR, FIRST_FAR, FIRST_WEIGHTED, FIRST_LAST = 7, 10, 2, 10, 1
 CODE = jnp.int16
-SCALE_ROWS = 16
-
-
-def exchange(pieces, axes):
-    return lax.all_to_all(pieces, axes, 0, 0, tiled=True)
+SCALE_ROWS = 8
+
+
+def exchange(pieces, axes, first):
+    groups = [[i ^ first for i in range(pieces.shape[0])]]
+    return lax.all_to_all(pieces, axes, 0, 0, tiled=True, axis_index_groups=groups)
 
 
 def in_hbm(array):
@@ -64,9 +66,9 @@
     largest = jnp.max(jnp.abs(values), axis=0, keepdims=True)
     exponent = jnp.floor(jnp.log2(jnp.maximum(largest, 2.0**-110))) + 1.0
     codes = jnp.round(values * jnp.exp2(14.0 - exponent))
-    out[(*at, pl.ds(0, rows))] = codes.astype(jnp.int32).astype(CODE)
     exponent = jnp.broadcast_to(exponent, (SCALE_ROWS, values.shape[1]))
-    out[(*at, pl.ds(rows, SCALE_ROWS))] = exponent.astype(jnp.int32).astype(CODE)
+    both = jnp.concatenate([codes, exponent], axis=0)
+    out[at] = both.astype(jnp.int32).astype(CODE)
 
 
 def decode(coded):
@@ -74,8 +76,8 @@
     rows -= SCALE_ROWS
     total = None
     for i in range(pieces):
-        exponent = coded[i, pl.ds(rows, SCALE_ROWS)].astype(jnp.float32)[:1]
-        part = coded[i, pl.ds(0, rows)].astype(jnp.float32) * jnp.exp2(exponent - 14.0)
+        both = coded[i].astype(jnp.float32)
+        part = both[:rows] * jnp.exp2(both[rows : rows + 1] - 14.0)
         total = part if total is None else total + part
     return total
 
@@ -111,7 +113,7 @@
 
             @pl.when(live)
             def _(j=j, k=k, row=row, col=col, scale=scale):
-                panel = jnp.concatenate([panels[col * per_col + i] for i in range(per_col)], axis=1)
+                panel = jnp.concatenate([panels[(col * per_col + i) ^ FIRST_PANELS] for i in range(per_col)], axis=1)
                 product = scale * lax.dot_general(
                     panel,
                     held[k, pl.ds(BAND * j, BAND), :],
@@ -123,11 +125,11 @@
                     total[where] = total[where] + product[:, t * piece : (t + 1) * piece]
 
     for c in range(out.shape[0]):
-        encode(total[c], out, (c,))
+        encode(total[c], out, c ^ FIRST_NEAR)
 
 
 def partial_kernel(coded, out):
-    encode(decode(coded), out, (0,))
+    encode(decode(coded), out, 0)
     for i in range(1, out.shape[0]):
         out[i] = out[0]
 
@@ -149,7 +151,7 @@
 
         @pl.when(live)
         def _(k=k, row=row, col=col, scale=scale):
-            rows = jnp.concatenate([weighted[row * per_row + i] for i in range(per_row)], axis=1)
+            rows = jnp.concatenate([weighted[(row * per_row + i) ^ FIRST_WEIGHTED] for i in range(per_row)], axis=1)
             for t in range(per_col):
                 product = scale * jnp.dot(
                     rows, held[k, :, pl.ds(own * t, own)], preferred_element_type=jnp.float32
@@ -157,7 +159,8 @@
                 where = col * per_col + t
                 total[where] = total[where] + product
 
-    out[...] = total[...].astype(jnp.bfloat16)
+    for o in range(out.shape[0]):
+        out[o ^ FIRST_LAST] = total[o].astype(jnp.bfloat16)
 
 
 def shards(
@@ -192,7 +195,7 @@
             pltpu.SemaphoreType.DMA((3,)),
         ],
     )
-    panels = exchange(copies, OBS)
+    panels = exchange(copies, OBS, FIRST_PANELS)
     coded = width + SCALE_ROWS
     pieces, held = call(
         forward_kernel,
@@ -211,16 +214,16 @@
         partial_kernel,
         pltpu.VMEM((lax.axis_size("zh"), coded, piece), CODE),
         [VMEM],
-        exchange(pieces, NEAR),
+        exchange(pieces, NEAR, FIRST_NEAR),
     )
     weighted = call(
         weigh_kernel,
         pltpu.VMEM((n_near, width, piece), bf16),
         [VMEM] * 2,
-        exchange(partial, "zh"),
+        exchange(partial, "zh", FIRST_FAR),
         noise_weight.reshape(n_near, piece),
     )
-    weighted = exchange(weighted, NEAR)
+    weighted = exchange(weighted, NEAR, FIRST_WEIGHTED)
     pieces = call(
         back_kernel,
         pltpu.VMEM((n_obs, width, own), bf16),
@@ -230,7 +233,7 @@
         held,
         scratch=[pltpu.VMEM((n_obs, width, own), f32)],
     )
-    summed = exchange(pieces, OBS).astype(f32).sum(0)
+    summed = exchange(pieces, OBS, FIRST_LAST).astype(f32).sum(0)
     return summed.T
 
 

time: 86.8 us -> 73.4 us (0.85)
  blocking collectives: 79.3 us -> 67.2 us
  Pallas kernels: 5.79 us -> 3.73 us
    all_to_all x5, blocking collectives: 79.3 us -> 67.2 us  [exchange(): lax.all_to_all(pieces, axes, 0, 0, tiled=True, axis_index_groups=groups)]
    pallas_call x5, Pallas kernels: 5.79 us -> 3.73 us  [call(): pl.pallas_call(kernel, out_shape=out, in_specs=in_specs, out_specs=out_sp...]
where the time goes in v5:
time: 73.4 us; the launch traced here: 72.3 us
  blocking collectives  67.2 us (92%)
  Pallas kernels  3.73 us (5%)
    all_to_all x5, blocking collectives, exchange(): lax.all_to_all(pieces, axes, 0, 0, tiled=True, axis_index_groups=groups)  67.2 us
    pallas_call x5, Pallas kernels, call(): pl.pallas_call(kernel, out_shape=out, in_specs=in_specs, out_specs=out_sp...  3.73 us

profile of v5, /device:TPU:1, one launch (start us, length us, event | category | flops | bytes accessed | tf_op | source)
XLA Modules:
  0.0 72.3 jit_solution(1050653644346782341)
XLA Ops:
  0.0 0.0 copy-start
  0.7 1.2 %shard_map.73 = (bf16[8,64,256]{2,1,0:T(8,128)(2,1)S(1)}, s32[7]{0:T(128)S(4)}) custom-call(s32[1,1]{1,0:T(1,128)S(6)} %copy.8.count, s32[1,2]{1,0:T(1,128)} %bitcast.8, s32[1,2]{1,0:T(1,128)} %bitcast.9, s32[1,2]{1,0:T(1,128)} %bitcast.10, bf16[64,256]{1,0:T(8,128)(2,1)} %bitcast.7), custom_call_target="tpu_custom_call" | custom-call | tf_op jit(solution)/shard_map/pallas_call | solution.py:31
  1.9 15.1 %all_to_all.25.panels = bf16[8,64,256]{2,1,0:T(8,128)(2,1)S(1)} all-to-all(bf16[8,64,256]{2,1,0:T(8,128)(2,1)S(1)} %get-tuple-element.10), channel_id=1, replica_groups={{7,6,5,4,3,2,1,0},{15,14,13,12,11,10,9,8},{23,22,21,20,19,18,17,16},{31..., dimensions={0} | all-to-all | bytes 524288 | tf_op jit(solution)/shard_map/all_to_all | solution.py:23
  17.0 2.3 %shard_map.74 = (s16[16,72,128]{2,1,0:T(8,128)(2,1)S(1)}, bf16[2,1024,1024]{2,1,0:T(8,128)(2,1)S(1)}) custom-call(s32[7]{0:T(128)S(4)} %get-tuple-element.9.info, bf16[8,64,256]{2,1,0:T(8,128)(2,1)S(1)} %all_to_all.25.panels, bf16[2,1,1024,1024]{3,2,1,0:T(8,128)(2,1)} %tiles.1), custom_call_target="tpu_custom_call" | custom-call | tf_op jit(solution)/shard_map/pallas_call | solution.py:31
  19.3 12.1 %all_to_all.26.coded = s16[16,72,128]{2,1,0:T(8,128)(2,1)S(1)} all-to-all(s16[16,72,128]{2,1,0:T(8,128)(2,1)S(1)} %get-tuple-element.11), channel_id=1, replica_groups={{272,280,256,264,400,408,384,392,16,24,0,8,144,152,128,136},{273,281,25..., dimensions={0} | all-to-all | bytes 589824 | tf_op jit(solution)/shard_map/all_to_all | solution.py:23
  31.4 0.1 shard_map.75
  31.6 15.9 %all_to_all.27.coded = s16[4,72,128]{2,1,0:T(8,128)(2,1)S(1)} all-to-all(s16[4,72,128]{2,1,0:T(8,128)(2,1)S(1)} %shard_map.75), channel_id=1, replica_groups={{64,96,0,32},{65,97,1,33},{66,98,2,34},{67,99,3,35},{68,100,4,36},{69,1..., dimensions={0} | all-to-all | bytes 147456 | tf_op jit(solution)/shard_map/all_to_all | solution.py:23
  47.5 0.0 copy-done
  47.5 9.8 %all_to_all.28.weighted = bf16[16,64,128]{2,1,0:T(8,128)(2,1)S(1)} all-to-all(bf16[16,64,128]{2,1,0:T(8,128)(2,1)S(1)} %shard_map.76), channel_id=1, replica_groups={{272,280,256,264,400,408,384,392,16,24,0,8,144,152,128,136},{273,281,25..., dimensions={0} | all-to-all | bytes 524288 | tf_op jit(solution)/shard_map/all_to_all | solution.py:23
  57.3 0.1 shard_map.77
  57.4 14.3 %all_to_all.29 = bf16[8,64,256]{2,1,0:T(8,128)(2,1)S(1)} all-to-all(bf16[8,64,256]{2,1,0:T(8,128)(2,1)S(1)} %shard_map.77), channel_id=1, replica_groups={{1,0,3,2,5,4,7,6},{9,8,11,10,13,12,15,14},{17,16,19,18,21,20,23,22},{25..., dimensions={0} | all-to-all | bytes 524288 | tf_op jit(solution)/shard_map/all_to_all | solution.py:23
  71.6 0.7 convert_reduce_fusion
  (1 shorter events, 0.0 us)
Async XLA Ops:
  0.0 47.5 %copy-start = (f32[2048]{0:T(1024)S(1)}, f32[2048]{0:T(1024)}, u32[]{:S(2)}) copy-start(f32[2048]{0:T(1024)} %param.13) | copy-start | bytes 24580

commit v6 on v5

--- a/solution.py
+++ b/solution.py
@@ -12,8 +12,8 @@
 SMEM = pl.BlockSpec(memory_space=pltpu.SMEM)
 HBM = pl.BlockSpec(memory_space=pltpu.HBM)
 PARAMS = pltpu.CompilerParams(vmem_limit_bytes=16 * 2**20)
-BAND = 256
-FIRST_PANELS, FIRST_NEAR, FIRST_FAR, FIRST_WEIGHTED, FIRST_LAST = 7, 10, 2, 10, 1
+BAND = 512
+FIRST_PANELS, FIRST_NEAR, FIRST_FAR, FIRST_WEIGHTED, FIRST_LAST = 7, 10, 2, 10, 5
 CODE = jnp.int16
 SCALE_ROWS = 8
 

time: 73.4 us -> 72.3 us (0.985)
  blocking collectives: 67.2 us -> 66.4 us
    all_to_all x5, blocking collectives: 67.2 us -> 66.4 us  [exchange(): lax.all_to_all(pieces, axes, 0, 0, tiled=True, axis_index_groups=groups)]
where the time goes in v6:
time: 72.3 us; the launch traced here: 71.5 us
  blocking collectives  66.4 us (92%)
  Pallas kernels  3.72 us (5%)
    all_to_all x5, blocking collectives, exchange(): lax.all_to_all(pieces, axes, 0, 0, tiled=True, axis_index_groups=groups)  66.4 us
    pallas_call x5, Pallas kernels, call(): pl.pallas_call(kernel, out_shape=out, in_specs=in_specs, out_specs=out_sp...  3.72 us

profile of v6, /device:TPU:1, one launch (start us, length us, event | category | flops | bytes accessed | tf_op | source)
XLA Modules:
  0.0 71.5 jit_solution(3137359559131172795)
XLA Ops:
  0.0 0.0 copy-start
  0.7 1.2 %shard_map.73 = (bf16[8,64,256]{2,1,0:T(8,128)(2,1)S(1)}, s32[7]{0:T(128)S(4)}) custom-call(s32[1,1]{1,0:T(1,128)S(6)} %copy.8.count, s32[1,2]{1,0:T(1,128)} %bitcast.8, s32[1,2]{1,0:T(1,128)} %bitcast.9, s32[1,2]{1,0:T(1,128)} %bitcast.10, bf16[64,256]{1,0:T(8,128)(2,1)} %bitcast.7), custom_call_target="tpu_custom_call" | custom-call | tf_op jit(solution)/shard_map/pallas_call | solution.py:31
  1.9 15.1 %all_to_all.25.panels = bf16[8,64,256]{2,1,0:T(8,128)(2,1)S(1)} all-to-all(bf16[8,64,256]{2,1,0:T(8,128)(2,1)S(1)} %get-tuple-element.10), channel_id=1, replica_groups={{7,6,5,4,3,2,1,0},{15,14,13,12,11,10,9,8},{23,22,21,20,19,18,17,16},{31..., dimensions={0} | all-to-all | bytes 524288 | tf_op jit(solution)/shard_map/all_to_all | solution.py:23
  17.0 2.3 %shard_map.74 = (s16[16,72,128]{2,1,0:T(8,128)(2,1)S(1)}, bf16[2,1024,1024]{2,1,0:T(8,128)(2,1)S(1)}) custom-call(s32[7]{0:T(128)S(4)} %get-tuple-element.9.info, bf16[8,64,256]{2,1,0:T(8,128)(2,1)S(1)} %all_to_all.25.panels, bf16[2,1,1024,1024]{3,2,1,0:T(8,128)(2,1)} %tiles.1), custom_call_target="tpu_custom_call" | custom-call | tf_op jit(solution)/shard_map/pallas_call | solution.py:31
  19.3 12.1 %all_to_all.26.coded = s16[16,72,128]{2,1,0:T(8,128)(2,1)S(1)} all-to-all(s16[16,72,128]{2,1,0:T(8,128)(2,1)S(1)} %get-tuple-element.11), channel_id=1, replica_groups={{272,280,256,264,400,408,384,392,16,24,0,8,144,152,128,136},{273,281,25..., dimensions={0} | all-to-all | bytes 589824 | tf_op jit(solution)/shard_map/all_to_all | solution.py:23
  31.4 0.1 shard_map.75
  31.6 14.7 %all_to_all.27.coded = s16[4,72,128]{2,1,0:T(8,128)(2,1)S(1)} all-to-all(s16[4,72,128]{2,1,0:T(8,128)(2,1)S(1)} %shard_map.75), channel_id=1, replica_groups={{64,96,0,32},{65,97,1,33},{66,98,2,34},{67,99,3,35},{68,100,4,36},{69,1..., dimensions={0} | all-to-all | bytes 147456 | tf_op jit(solution)/shard_map/all_to_all | solution.py:23
  46.3 0.0 copy-done
  46.3 9.8 %all_to_all.28.weighted = bf16[16,64,128]{2,1,0:T(8,128)(2,1)S(1)} all-to-all(bf16[16,64,128]{2,1,0:T(8,128)(2,1)S(1)} %shard_map.76), channel_id=1, replica_groups={{272,280,256,264,400,408,384,392,16,24,0,8,144,152,128,136},{273,281,25..., dimensions={0} | all-to-all | bytes 524288 | tf_op jit(solution)/shard_map/all_to_all | solution.py:23
  56.2 0.1 shard_map.77
  56.2 14.6 %all_to_all.29 = bf16[8,64,256]{2,1,0:T(8,128)(2,1)S(1)} all-to-all(bf16[8,64,256]{2,1,0:T(8,128)(2,1)S(1)} %shard_map.77), channel_id=1, replica_groups={{5,4,7,6,1,0,3,2},{13,12,15,14,9,8,11,10},{21,20,23,22,17,16,19,18},{29..., dimensions={0} | all-to-all | bytes 524288 | tf_op jit(solution)/shard_map/all_to_all | solution.py:23
  70.8 0.7 convert_reduce_fusion
  (1 shorter events, 0.0 us)
Async XLA Ops:
  0.0 46.3 %copy-start = (f32[2048]{0:T(1024)S(1)}, f32[2048]{0:T(1024)}, u32[]{:S(2)}) copy-start(f32[2048]{0:T(1024)} %param.13) | copy-start | bytes 24580

commit v7 on v6

--- a/solution.py
+++ b/solution.py
@@ -43,9 +43,7 @@
 
 
 def start_kernel(count, row, col, exponent, probes, copies, info, held, arrived, read):
-    sent = [
-        pltpu.make_async_copy(probes, copies.at[i], arrived.at[i]) for i in range(copies.shape[0])
-    ]
+    sent = [pltpu.make_async_copy(probes, copies.at[0], arrived.at[0])]
     sent += [
         pltpu.make_async_copy(source, held.at[i], read.at[i])
         for i, source in enumerate((row, col, exponent))
@@ -54,6 +52,8 @@
         copy.start()
     for copy in sent:
         copy.wait()
+    for i in range(1, copies.shape[0]):
+        copies[i] = copies[0]
     slots = row.shape[1]
     info[0] = count[0, 0]
     for i in range(3):

time: 72.3 us -> 72 us (level)
  blocking collectives: 66.4 us -> 64.6 us
  Pallas kernels: 3.72 us -> 5.18 us
    all_to_all x5, blocking collectives: 66.4 us -> 64.6 us  [exchange(): lax.all_to_all(pieces, axes, 0, 0, tiled=True, axis_index_groups=groups)]
    pallas_call x5, Pallas kernels: 3.72 us -> 5.18 us  [call(): pl.pallas_call(kernel, out_shape=out, in_specs=in_specs, out_specs=out_sp...]
where the time goes in v7:
time: 72 us; the launch traced here: 71.2 us
  blocking collectives  64.6 us (90%)
  Pallas kernels  5.18 us (7%)
    all_to_all x5, blocking collectives, exchange(): lax.all_to_all(pieces, axes, 0, 0, tiled=True, axis_index_groups=groups)  64.6 us
    pallas_call x5, Pallas kernels, call(): pl.pallas_call(kernel, out_shape=out, in_specs=in_specs, out_specs=out_sp...  5.18 us

profile of v7, /device:TPU:1, one launch (start us, length us, event | category | flops | bytes accessed | tf_op | source)
XLA Modules:
  0.0 71.2 jit_solution(13496527535430932133)
XLA Ops:
  0.0 0.0 copy-start
  0.7 0.9 %shard_map.73 = (bf16[8,64,256]{2,1,0:T(8,128)(2,1)S(1)}, s32[7]{0:T(128)S(4)}) custom-call(s32[1,1]{1,0:T(1,128)S(6)} %copy.8.count, s32[1,2]{1,0:T(1,128)} %bitcast.8, s32[1,2]{1,0:T(1,128)} %bitcast.9, s32[1,2]{1,0:T(1,128)} %bitcast.10, bf16[64,256]{1,0:T(8,128)(2,1)} %bitcast.7), custom_call_target="tpu_custom_call" | custom-call | tf_op jit(solution)/shard_map/pallas_call | solution.py:31
  1.6 15.1 %all_to_all.25.panels = bf16[8,64,256]{2,1,0:T(8,128)(2,1)S(1)} all-to-all(bf16[8,64,256]{2,1,0:T(8,128)(2,1)S(1)} %get-tuple-element.10), channel_id=1, replica_groups={{7,6,5,4,3,2,1,0},{15,14,13,12,11,10,9,8},{23,22,21,20,19,18,17,16},{31..., dimensions={0} | all-to-all | bytes 524288 | tf_op jit(solution)/shard_map/all_to_all | solution.py:23
  16.7 3.2 %shard_map.74 = (s16[16,72,128]{2,1,0:T(8,128)(2,1)S(1)}, bf16[2,1024,1024]{2,1,0:T(8,128)(2,1)S(1)}) custom-call(s32[7]{0:T(128)S(4)} %get-tuple-element.9.info, bf16[8,64,256]{2,1,0:T(8,128)(2,1)S(1)} %all_to_all.25.panels, bf16[2,1,1024,1024]{3,2,1,0:T(8,128)(2,1)} %tiles.1), custom_call_target="tpu_custom_call" | custom-call | tf_op jit(solution)/shard_map/pallas_call | solution.py:31
  19.9 12.4 %all_to_all.26.coded = s16[16,72,128]{2,1,0:T(8,128)(2,1)S(1)} all-to-all(s16[16,72,128]{2,1,0:T(8,128)(2,1)S(1)} %get-tuple-element.11), channel_id=1, replica_groups={{272,280,256,264,400,408,384,392,16,24,0,8,144,152,128,136},{273,281,25..., dimensions={0} | all-to-all | bytes 589824 | tf_op jit(solution)/shard_map/all_to_all | solution.py:23
  32.3 0.1 shard_map.75
  32.4 14.6 %all_to_all.27.coded = s16[4,72,128]{2,1,0:T(8,128)(2,1)S(1)} all-to-all(s16[4,72,128]{2,1,0:T(8,128)(2,1)S(1)} %shard_map.75), channel_id=1, replica_groups={{64,96,0,32},{65,97,1,33},{66,98,2,34},{67,99,3,35},{68,100,4,36},{69,1..., dimensions={0} | all-to-all | bytes 147456 | tf_op jit(solution)/shard_map/all_to_all | solution.py:23
  47.1 0.0 copy-done
  47.1 9.7 %all_to_all.28.weighted = bf16[16,64,128]{2,1,0:T(8,128)(2,1)S(1)} all-to-all(bf16[16,64,128]{2,1,0:T(8,128)(2,1)S(1)} %shard_map.76), channel_id=1, replica_groups={{272,280,256,264,400,408,384,392,16,24,0,8,144,152,128,136},{273,281,25..., dimensions={0} | all-to-all | bytes 524288 | tf_op jit(solution)/shard_map/all_to_all | solution.py:23
  56.9 0.9 %shard_map.77 = bf16[8,64,256]{2,1,0:T(8,128)(2,1)S(1)} custom-call(s32[7]{0:T(128)S(4)} %get-tuple-element.9.info, bf16[16,64,128]{2,1,0:T(8,128)(2,1)S(1)} %all_to_all.28.weighted, bf16[2,1024,1024]{2,1,0:T(8,128)(2,1)S(1)} %get-tuple-element.12.held), custom_call_target="tpu_custom_call" | custom-call | tf_op jit(solution)/shard_map/pallas_call | solution.py:31
  57.8 12.7 %all_to_all.29 = bf16[8,64,256]{2,1,0:T(8,128)(2,1)S(1)} all-to-all(bf16[8,64,256]{2,1,0:T(8,128)(2,1)S(1)} %shard_map.77), channel_id=1, replica_groups={{5,4,7,6,1,0,3,2},{13,12,15,14,9,8,11,10},{21,20,23,22,17,16,19,18},{29..., dimensions={0} | all-to-all | bytes 524288 | tf_op jit(solution)/shard_map/all_to_all | solution.py:23
  70.5 0.7 convert_reduce_fusion
  (1 shorter events, 0.0 us)
Async XLA Ops:
  0.0 47.1 %copy-start = (f32[2048]{0:T(1024)S(1)}, f32[2048]{0:T(1024)}, u32[]{:S(2)}) copy-start(f32[2048]{0:T(1024)} %param.13) | copy-start | bytes 24580
